TPU v7x, 32 devices: a whole 2x2x4 slice. The times are simulated.
32 devices in a mesh: bag: 4 (over y, core), head: 8 (over z, x).
Axes of the slice: x: 2, y: 2, z: 4, core: 2. Of those that a mesh axis runs over, the one named last changes fastest.
Arguments:
- dout: bfloat16 [4096, 6144], P(('bag', 'head')), may hold values from -6 to 6
- destination: int32 [4096], P(('bag', 'head')), may hold values from 0 to 4095, as said below
- q_bag: bfloat16 [4096, 6144], P(('bag', 'head')), may hold values from -32 to 32
- k_bag: bfloat16 [4096, 6144], P(('bag', 'head')), may hold values from -32 to 32
- v_bag: bfloat16 [4096, 6144], P(('bag', 'head')), may hold values from -6 to 6
- seq_ids: int32 [4, 1024], P('bag'), may hold values from 0 to 2, never falling along the last dimension, each value on 1 to 768 neighbouring positions
Outputs:
- dq_bag: bfloat16 [4096, 6144], P(('bag', 'head'))
- dk_bag: bfloat16 [4096, 6144], P(('bag', 'head'))
- dv_bag: bfloat16 [4096, 6144], P(('bag', 'head'))
Inputs may be any that keep to these rules, and one draw needn't show every extreme that they name: destination is a permutation. A row at home index i goes to a bag row held at the same index along head: destination // 128 % 8 equals i // 128 % 8. The rows of one device go to at most four bags, at most 64 of them to one bag, and in every draw some device sends exactly 64 rows to some bag.
All inputs are finite; a program needn't handle non-finite values.
Results may differ from a plain program's by a relative error of at most 0.011.
Values may be sent and summed in bfloat16 or wider, within the bound.
A program may use at most 128 MiB of HBM per device.

v0:
```python
import functools

import jax
import jax.numpy as jnp
from jax import lax
from jax.experimental import pallas as pl
from jax.experimental.pallas import tpu as pltpu
from jax.sharding import PartitionSpec as P

HEAD_DIM = 128
CAP = 64
MESH = pl.DeviceIdType.MESH
F32 = jnp.float32
BF16 = jnp.bfloat16
CONTRACT_LAST = (((1,), (1,)), ((), ()))
CONTRACT_FIRST = (((0,), (0,)), ((), ()))


def rank_matrix(labels, bag, bag_rows):
    rows = labels.shape[1]
    inside = (labels >= bag * bag_rows) & (labels < (bag + 1) * bag_rows)
    earlier = lax.broadcasted_iota(jnp.int32, (rows, rows), 0) < lax.broadcasted_iota(
        jnp.int32, (rows, rows), 1
    )
    ranks = jnp.dot(
        jnp.where(inside, 1.0, 0.0).astype(BF16),
        jnp.where(earlier, 1.0, 0.0).astype(BF16),
        preferred_element_type=F32,
    )
    ranks = jnp.where(inside, ranks, -1.0)[0:1, :]
    slots = lax.broadcasted_iota(jnp.int32, (CAP, rows), 0).astype(F32)
    return jnp.where(slots == ranks, 1.0, 0.0).astype(BF16)


def kernel(
    bags,
    groups,
    heads,
    early,
    block,
    dout_ref,
    labels_ref,
    q_ref,
    k_ref,
    v_ref,
    seq_row_ref,
    seq_col_ref,
    dq_ref,
    dk_ref,
    dv_ref,
    packed,
    arrived,
    other_labels,
    grad_rows,
    qb,
    kb,
    vb,
    gb,
    dqb,
    dkb,
    dvb,
    dk_sum,
    dv_sum,
    in_send,
    in_recv,
    out_send,
    out_recv,
    bag_send,
    bag_recv,
    label_send,
    label_recv,
):
    my_bag = lax.axis_index("bag")
    me = lax.axis_index("head")
    rows, width = dout_ref.shape
    bag_rows = rows * groups
    local = heads * HEAD_DIM
    my_rows = pl.ds(pl.multiple_of(me * rows, rows), rows)

    barrier = pltpu.get_barrier_semaphore()
    for t in range(1, groups):
        pl.semaphore_signal(
            barrier, inc=1, device_id=(my_bag, lax.rem(me + t, groups)), device_id_type=MESH
        )
    for t in range(1, bags):
        pl.semaphore_signal(
            barrier, inc=1, device_id=(lax.rem(my_bag + t, bags), me), device_id_type=MESH
        )
    pl.semaphore_wait(barrier, groups + bags - 2)

    def columns(owner, h):
        return pl.ds(pl.multiple_of(owner * local + h * HEAD_DIM, HEAD_DIM), HEAD_DIM)

    def send_head(source, target, index, h):
        for t in range(1, groups):
            peer = lax.rem(me + t, groups)
            pltpu.make_async_remote_copy(
                src_ref=source.at[:, columns(peer, h)],
                dst_ref=target.at[h, my_rows, :],
                send_sem=in_send.at[index],
                recv_sem=in_recv.at[index, h],
                device_id=(my_bag, peer),
                device_id_type=MESH,
            ).start()
        pltpu.make_async_copy(
            source.at[:, columns(me, h)], target.at[h, my_rows, :], in_recv.at[index, h]
        ).start()

    def send_qkv(h, carry):
        send_head(q_ref, qb, 0, h)
        send_head(k_ref, kb, 1, h)
        send_head(v_ref, vb, 2, h)
        return carry

    lax.fori_loop(0, 1, send_qkv, 0)

    label_copies, bag_copies = [], []
    labels = labels_ref[...]
    for t in range(1, bags):
        copy = pltpu.make_async_remote_copy(
            src_ref=labels_ref,
            dst_ref=other_labels.at[t - 1],
            send_sem=label_send.at[t - 1],
            recv_sem=label_recv.at[t - 1],
            device_id=(lax.rem(my_bag + t, bags), me),
            device_id_type=MESH,
        )
        copy.start()
        label_copies.append(copy)
    for t in list(range(1, bags)) + [0]:
        bag = lax.rem(my_bag + t, bags)
        pick = rank_matrix(labels, bag, bag_rows)

        def pack(i, carry):
            cols = pl.ds(pl.multiple_of(i * local, local), local)
            packed[t, :, cols] = jnp.dot(
                pick, dout_ref[:, cols], preferred_element_type=F32
            ).astype(BF16)
            return carry

        lax.fori_loop(0, width // local, pack, 0)
        if t:
            copy = pltpu.make_async_remote_copy(
                src_ref=packed.at[t],
                dst_ref=arrived.at[t - 1],
                send_sem=bag_send.at[t - 1],
                recv_sem=bag_recv.at[t - 1],
                device_id=(bag, me),
                device_id_type=MESH,
            )
            copy.start()
            bag_copies.append(copy)

    lax.fori_loop(1, early, send_qkv, 0)

    first_row = my_bag * bag_rows + me * rows
    row_ids = first_row + lax.broadcasted_iota(jnp.int32, (rows, rows), 0)
    places = []
    for t in range(bags):
        if t:
            label_copies[t - 1].wait()
            theirs = other_labels[t - 1]
        else:
            theirs = labels
        hit = jnp.where(row_ids == theirs[0:1, :], 1.0, 0.0).astype(BF16)
        places.append(
            lax.dot_general(
                hit,
                rank_matrix(theirs, my_bag, bag_rows),
                CONTRACT_LAST,
                preferred_element_type=F32,
            ).astype(BF16)
        )
    for copy in bag_copies:
        copy.wait()

    def place(i, carry):
        cols = pl.ds(pl.multiple_of(i * local, local), local)
        total = jnp.dot(places[0], packed[0, :, cols], preferred_element_type=F32)
        for t in range(1, bags):
            total += jnp.dot(places[t], arrived[t - 1, :, cols], preferred_element_type=F32)
        grad_rows[:, cols] = total.astype(BF16)
        return carry

    lax.fori_loop(0, width // local, place, 0)

    def send_grad(h, carry):
        send_head(grad_rows, gb, 3, h)
        return carry

    def send_all(h, carry):
        return send_grad(h, send_qkv(h, carry))

    lax.fori_loop(0, early, send_grad, 0)
    lax.fori_loop(early, heads, send_all, 0)

    scale = HEAD_DIM ** (-0.5)
    exp2_scale = scale * 1.4426950408889634

    def one_head(h, carry):
        for index, buffer in enumerate((qb, kb, vb, gb)):
            pltpu.make_async_copy(buffer.at[h], buffer.at[h], in_recv.at[index, h]).wait()
        dk_sum[...] = jnp.zeros_like(dk_sum)
        dv_sum[...] = jnp.zeros_like(dv_sum)

        def one_block(i, inner):
            here = pl.ds(pl.multiple_of(i * block, block), block)
            query, grad = qb[h, here, :], gb[h, here, :]
            keys, values = kb[h], vb[h]
            scores = lax.dot_general(keys, query, CONTRACT_LAST, preferred_element_type=F32)
            same = seq_col_ref[...] == seq_row_ref[:, here]
            scores = jnp.where(same, scores, -jnp.inf)
            top = jnp.max(scores, axis=0, keepdims=True)
            exponent = jnp.exp2((scores - top) * exp2_scale)
            probs = exponent * (1.0 / jnp.sum(exponent, axis=0, keepdims=True))
            dv_sum[...] += jnp.dot(probs.astype(BF16), grad, preferred_element_type=F32)
            dprobs = lax.dot_general(values, grad, CONTRACT_LAST, preferred_element_type=F32)
            delta = jnp.sum(probs * dprobs, axis=0, keepdims=True)
            dscores = (probs * (dprobs - delta) * scale).astype(BF16)
            dk_sum[...] += jnp.dot(dscores, query, preferred_element_type=F32)
            dqb[h, here, :] = lax.dot_general(
                dscores, keys, CONTRACT_FIRST, preferred_element_type=F32
            ).astype(BF16)
            return inner

        lax.fori_loop(0, bag_rows // block, one_block, 0)
        dkb[h] = dk_sum[...].astype(BF16)
        dvb[h] = dv_sum[...].astype(BF16)
        for index, (source, target) in enumerate(((dqb, dq_ref), (dkb, dk_ref), (dvb, dv_ref))):
            for t in range(1, groups):
                peer = lax.rem(me + t, groups)
                theirs = pl.ds(pl.multiple_of(peer * rows, rows), rows)
                pltpu.make_async_remote_copy(
                    src_ref=source.at[h, theirs, :],
                    dst_ref=target.at[:, columns(me, h)],
                    send_sem=out_send.at[index],
                    recv_sem=out_recv.at[index],
                    device_id=(my_bag, peer),
                    device_id_type=MESH,
                ).start()
            pltpu.make_async_copy(
                source.at[h, my_rows, :], target.at[:, columns(me, h)], out_recv.at[index]
            ).start()
        return carry

    lax.fori_loop(0, heads, one_head, 0)

    sent = grad_rows.at[:, pl.ds(0, (groups - 1) * local)]
    for index in range(4):
        pltpu.make_async_copy(sent, sent, in_send.at[index]).wait()
    for index, target in enumerate((dq_ref, dk_ref, dv_ref)):
        pltpu.make_async_copy(sent, sent, out_send.at[index]).wait()
        pltpu.make_async_copy(target, target, out_recv.at[index]).wait()


def per_device(dout, destination, q_bag, k_bag, v_bag, seq_ids):
    rows, width = dout.shape
    bags = lax.axis_size("bag")
    groups = lax.axis_size("head")
    bag_rows = rows * groups
    heads = width // HEAD_DIM // groups
    early = (heads + 1) // 2
    block = min(256, bag_rows)
    labels = jnp.broadcast_to(destination[None, :], (8, rows))
    whole = pl.BlockSpec(memory_space=pltpu.VMEM)
    far = pl.BlockSpec(memory_space=pl.ANY)
    sems = pltpu.SemaphoreType.DMA
    head_buffer = pltpu.VMEM((heads, bag_rows, HEAD_DIM), BF16)
    return pl.pallas_call(
        functools.partial(kernel, bags, groups, heads, early, block),
        out_shape=[jax.ShapeDtypeStruct((rows, width), BF16)] * 3,
        in_specs=[whole, whole, far, far, far, whole, whole],
        out_specs=[far, far, far],
        scratch_shapes=[
            pltpu.VMEM((bags, CAP, width), BF16),
            pltpu.VMEM((bags - 1, CAP, width), BF16),
            pltpu.VMEM((bags - 1, 8, rows), jnp.int32),
            pltpu.VMEM((rows, width), BF16),
        ]
        + [head_buffer] * 7
        + [
            pltpu.VMEM((bag_rows, HEAD_DIM), F32),
            pltpu.VMEM((bag_rows, HEAD_DIM), F32),
            sems((4,)),
            sems((4, heads)),
            sems((3,)),
            sems((3,)),
            sems((bags - 1,)),
            sems((bags - 1,)),
            sems((bags - 1,)),
            sems((bags - 1,)),
        ],
        compiler_params=pltpu.CompilerParams(
            collective_id=0, has_side_effects=True, vmem_limit_bytes=56 * 1024 * 1024
        ),
    )(dout, labels, q_bag, k_bag, v_bag, seq_ids, seq_ids.reshape(bag_rows, 1))


def solution(mesh):
    placed = (
        P(("bag", "head"), None),
        P(("bag", "head")),
        P(("bag", "head"), None),
        P(("bag", "head"), None),
        P(("bag", "head"), None),
        P("bag", None),
    )
    return jax.shard_map(
        per_device,
        mesh=mesh,
        in_specs=placed,
        out_specs=(P(("bag", "head"), None),) * 3,
        check_vma=False,
    )
```

profile of v0, /device:TPU:0, one launch (start us, length us, event | category | flops | bytes accessed | tf_op | source)
XLA Modules:
  0.0 253.7 jit_solution(17676200560904109901)
XLA Ops:
  0.6 1.2 broadcast_in_dim.2.labels_ref
  1.9 1.7 copy.9.seq_col_ref
  3.6 244.2 %shard_map.85 = (bf16[128,6144]{1,0:T(8,128)(2,1)}, bf16[128,6144]{1,0:T(8,128)(2,1)}, bf16[128,6144]{1,0:T(8,128)(2,1)}) custom-call(bf16[128,6144]{1,0:T(8,128)(2,1)} %dout_ref.1, s32[8,128]{1,0:T(8,128)} %broadcast_in_dim.2.labels_ref, bf16[128,6144]{1,0:T(8,128)(2,1)} %q_ref.1, bf16[128,6144]{1,0:T(8,128)(2,1)} %k_ref.1, bf16[128,6144]{1,0:T(8,128)(2,1)} %v_ref.1, ...), custom_call_target="tpu_custom_call" | custom-call | tf_op jit(solution)/shard_map/pallas_call | solution.py:269
  247.8 0.0 copy-start.1
  247.8 2.8 %copy.13 = bf16[128,6144]{1,0:T(8,128)(2,1)} copy(bf16[128,6144]{1,0:T(8,128)(2,1)} %get-tuple-element.6) | data formatting | bytes 3145728
  250.6 0.0 copy-done.1
  250.6 0.0 copy-start
  250.6 1.1 copy.14
  251.8 0.8 copy-done
  252.6 1.1 copy.15
Async XLA Ops:
  247.8 2.8 %copy-start.1 = (bf16[128,6144]{1,0:T(8,128)(2,1)S(1)}, bf16[128,6144]{1,0:T(8,128)(2,1)}, u32[]{:S(2)}) copy-start(bf16[128,6144]{1,0:T(8,128)(2,1)} %get-tuple-element.7) | copy-start | bytes 4718596
  250.6 2.0 copy-start
where the time goes:
time: 254 us
  Pallas kernels  244 us (96%)
  local copies, waits for them, and re-layouts  8.88 us (3%)
    pallas_call x1, Pallas kernels, per_device(): pl.pallas_call(functools.partial(kernel, bags, groups, heads, early, bloc...  244 us
    unnamed x7, local copies, waits for them, and re-layouts  5.93 us

commit v1 on v0

v1 whole, which is shorter than its diff:
```python
import functools

import jax
import jax.numpy as jnp
from jax import lax
from jax.experimental import pallas as pl
from jax.experimental.pallas import tpu as pltpu
from jax.sharding import PartitionSpec as P

HEAD_DIM = 128
CAP = 64
MESH = pl.DeviceIdType.MESH
F32 = jnp.float32
BF16 = jnp.bfloat16
NEVER = -1e30
CONTRACT_LAST = (((1,), (1,)), ((), ()))
CONTRACT_FIRST = (((0,), (0,)), ((), ()))


def rank_matrix(labels, bag, bag_rows):
    rows = labels.shape[1]
    inside = (labels >= bag * bag_rows) & (labels < (bag + 1) * bag_rows)
    earlier = lax.broadcasted_iota(jnp.int32, (rows, rows), 0) < lax.broadcasted_iota(
        jnp.int32, (rows, rows), 1
    )
    ranks = jnp.dot(
        jnp.where(inside, 1.0, 0.0).astype(BF16),
        jnp.where(earlier, 1.0, 0.0).astype(BF16),
        preferred_element_type=F32,
    )
    ranks = jnp.where(inside, ranks, -1.0)[0:1, :]
    slots = lax.broadcasted_iota(jnp.int32, (CAP, rows), 0).astype(F32)
    return jnp.where(slots == ranks, 1.0, 0.0).astype(BF16)


def kernel(
    bags,
    groups,
    heads,
    early,
    block,
    dout_ref,
    labels_ref,
    q_ref,
    k_ref,
    v_ref,
    seq_row_ref,
    seq_col_ref,
    dq_ref,
    dk_ref,
    dv_ref,
    packed,
    arrived,
    other_labels,
    grad_rows,
    qb,
    gb,
    kb,
    vb,
    dq_own,
    dq_out,
    dq_in,
    dqb,
    dkb,
    dvb,
    my_stats,
    pair_stats,
    dk_sum,
    dv_sum,
    in_send,
    in_recv,
    pair_send,
    pair_recv,
    stat_send,
    stat_recv,
    part_send,
    part_recv,
    out_send,
    out_recv,
    bag_send,
    bag_recv,
    label_send,
    label_recv,
):
    my_bag = lax.axis_index("bag")
    me = lax.axis_index("head")
    half = groups // 2
    side = me // half
    place_in = lax.rem(me, half)
    partner = (my_bag, lax.rem(me + half, groups))
    rows, width = dout_ref.shape
    bag_rows = rows * groups
    half_rows = rows * half
    local = heads * HEAD_DIM
    my_rows = pl.ds(pl.multiple_of(place_in * rows, rows), rows)

    def mate(t):
        at = lax.rem(place_in + t, half)
        return at, (my_bag, side * half + at)

    barrier = pltpu.get_barrier_semaphore()
    for t in range(1, half):
        pl.semaphore_signal(barrier, inc=1, device_id=mate(t)[1], device_id_type=MESH)
    pl.semaphore_signal(barrier, inc=1, device_id=partner, device_id_type=MESH)
    for t in range(1, bags):
        pl.semaphore_signal(
            barrier, inc=1, device_id=(lax.rem(my_bag + t, bags), me), device_id_type=MESH
        )
    pl.semaphore_wait(barrier, half + bags - 1)

    def columns(owner, h):
        return pl.ds(pl.multiple_of(owner * local + h * HEAD_DIM, HEAD_DIM), HEAD_DIM)

    def send_head(source, target, index, h):
        for t in range(1, half):
            at, device = mate(t)
            pltpu.make_async_remote_copy(
                src_ref=source.at[:, columns(at, h)],
                dst_ref=target.at[h, my_rows, :],
                send_sem=in_send.at[index],
                recv_sem=in_recv.at[index, h],
                device_id=device,
                device_id_type=MESH,
            ).start()
        pltpu.make_async_copy(
            source.at[:, columns(place_in, h)], target.at[h, my_rows, :], in_recv.at[index, h]
        ).start()

    def wait_head(buffer, index, h):
        pltpu.make_async_copy(buffer.at[h], buffer.at[h], in_recv.at[index, h]).wait()

    def to_partner(source, target, send_sem, recv_sem):
        pltpu.make_async_remote_copy(
            src_ref=source,
            dst_ref=target,
            send_sem=send_sem,
            recv_sem=recv_sem,
            device_id=partner,
            device_id_type=MESH,
        ).start()

    def send_q(h, carry):
        send_head(q_ref, qb.at[0], 0, h)
        return carry

    def send_kv(h, carry):
        send_head(k_ref, kb, 1, h)
        send_head(v_ref, vb, 2, h)
        return carry

    def send_grad(h, carry):
        send_head(grad_rows, gb.at[0], 3, h)
        return carry

    def relay_q(h, carry):
        wait_head(qb.at[0], 0, h)
        to_partner(qb.at[0, h], qb.at[1, h], pair_send.at[0], pair_recv.at[0, h])
        return carry

    def relay_grad(h, carry):
        wait_head(gb.at[0], 3, h)
        to_partner(gb.at[0, h], gb.at[1, h], pair_send.at[1], pair_recv.at[1, h])
        return carry

    lax.fori_loop(0, heads, send_q, 0)

    label_copies, bag_copies = [], []
    labels = labels_ref[...]
    for t in range(1, bags):
        copy = pltpu.make_async_remote_copy(
            src_ref=labels_ref,
            dst_ref=other_labels.at[t - 1],
            send_sem=label_send.at[t - 1],
            recv_sem=label_recv.at[t - 1],
            device_id=(lax.rem(my_bag + t, bags), me),
            device_id_type=MESH,
        )
        copy.start()
        label_copies.append(copy)
    for t in list(range(1, bags)) + [0]:
        bag = lax.rem(my_bag + t, bags)
        pick = rank_matrix(labels, bag, bag_rows)

        def pack(i, carry):
            cols = pl.ds(pl.multiple_of(i * local, local), local)
            packed[t, :, cols] = jnp.dot(
                pick, dout_ref[:, cols], preferred_element_type=F32
            ).astype(BF16)
            return carry

        lax.fori_loop(0, width // local, pack, 0)
        if t:
            copy = pltpu.make_async_remote_copy(
                src_ref=packed.at[t],
                dst_ref=arrived.at[t - 1],
                send_sem=bag_send.at[t - 1],
                recv_sem=bag_recv.at[t - 1],
                device_id=(bag, me),
                device_id_type=MESH,
            )
            copy.start()
            bag_copies.append(copy)

    lax.fori_loop(0, early, relay_q, 0)
    lax.fori_loop(0, early, send_kv, 0)
    lax.fori_loop(early, heads, relay_q, 0)

    first_row = my_bag * bag_rows + me * rows
    row_ids = first_row + lax.broadcasted_iota(jnp.int32, (rows, rows), 0)
    places = []
    for t in range(bags):
        if t:
            label_copies[t - 1].wait()
            theirs = other_labels[t - 1]
        else:
            theirs = labels
        hit = jnp.where(row_ids == theirs[0:1, :], 1.0, 0.0).astype(BF16)
        places.append(
            lax.dot_general(
                hit,
                rank_matrix(theirs, my_bag, bag_rows),
                CONTRACT_LAST,
                preferred_element_type=F32,
            ).astype(BF16)
        )
    for copy in bag_copies:
        copy.wait()

    def place(i, carry):
        cols = pl.ds(pl.multiple_of(i * local, local), local)
        total = jnp.dot(places[0], packed[0, :, cols], preferred_element_type=F32)
        for t in range(1, bags):
            total += jnp.dot(places[t], arrived[t - 1, :, cols], preferred_element_type=F32)
        grad_rows[:, cols] = total.astype(BF16)
        return carry

    lax.fori_loop(0, width // local, place, 0)

    lax.fori_loop(0, heads, send_grad, 0)
    lax.fori_loop(early, heads, send_kv, 0)

    scale = HEAD_DIM ** (-0.5)
    exp2_scale = scale * 1.4426950408889634
    blocks = half_rows // block
    key_labels = seq_col_ref.at[pl.ds(pl.multiple_of(side * half_rows, half_rows), half_rows), :]

    def block_parts(part, i, h):
        here = pl.ds(pl.multiple_of(i * block, block), block)
        other = side + part - 2 * side * part
        query_at = pl.ds(pl.multiple_of(other * half_rows + i * block, block), block)
        query, grad = qb[part, h, here, :], gb[part, h, here, :]
        scores = lax.dot_general(kb[h], query, CONTRACT_LAST, preferred_element_type=F32)
        scores = jnp.where(key_labels[...] == seq_row_ref[:, query_at], scores, NEVER)
        dprobs = lax.dot_general(vb[h], grad, CONTRACT_LAST, preferred_element_type=F32)
        return here, query_at, query, grad, scores, dprobs

    def statistics(h):
        wait_head(kb, 1, h)
        wait_head(vb, 2, h)
        for index, buffer in enumerate((qb, gb)):
            ref = buffer.at[1, h]
            pltpu.make_async_copy(ref, ref, pair_recv.at[index, h]).wait()

        for part in (1, 0):

            def one_block(i, inner):
                _, query_at, _, _, scores, dprobs = block_parts(part, i, h)
                top = jnp.max(scores, axis=0, keepdims=True)
                exponent = jnp.exp2((scores - top) * exp2_scale)
                my_stats[h, 0:1, query_at] = top
                my_stats[h, 1:2, query_at] = jnp.sum(exponent, axis=0, keepdims=True)
                my_stats[h, 2:3, query_at] = jnp.sum(exponent * dprobs, axis=0, keepdims=True)
                return inner

            lax.fori_loop(0, blocks, one_block, 0)
        to_partner(my_stats.at[h], pair_stats.at[h], stat_send.at[0], stat_recv.at[h])

    def send_out(source, target, index, h):
        for t in range(1, half):
            at, device = mate(t)
            theirs = pl.ds(pl.multiple_of(at * rows, rows), rows)
            pltpu.make_async_remote_copy(
                src_ref=source.at[h, theirs, :],
                dst_ref=target.at[:, columns(place_in, h)],
                send_sem=out_send.at[index],
                recv_sem=out_recv.at[index],
                device_id=device,
                device_id_type=MESH,
            ).start()
        pltpu.make_async_copy(
            source.at[h, my_rows, :], target.at[:, columns(place_in, h)], out_recv.at[index]
        ).start()

    def gradients(h):
        stats = pair_stats.at[h]
        pltpu.make_async_copy(stats, stats, stat_recv.at[h]).wait()
        dk_sum[...] = jnp.zeros_like(dk_sum)
        dv_sum[...] = jnp.zeros_like(dv_sum)

        for part in (1, 0):

            def one_block(i, inner):
                here, query_at, query, grad, scores, dprobs = block_parts(part, i, h)
                top_a, top_b = my_stats[h, 0:1, query_at], pair_stats[h, 0:1, query_at]
                top = jnp.maximum(top_a, top_b)
                weight_a = jnp.exp2((top_a - top) * exp2_scale)
                weight_b = jnp.exp2((top_b - top) * exp2_scale)
                inverse = 1.0 / (
                    my_stats[h, 1:2, query_at] * weight_a + pair_stats[h, 1:2, query_at] * weight_b
                )
                delta = inverse * (
                    my_stats[h, 2:3, query_at] * weight_a + pair_stats[h, 2:3, query_at] * weight_b
                )
                probs = jnp.exp2((scores - top) * exp2_scale) * inverse
                dv_sum[...] += jnp.dot(probs.astype(BF16), grad, preferred_element_type=F32)
                dscores = (probs * (dprobs - delta)).astype(BF16)
                dk_sum[...] += jnp.dot(dscores, query, preferred_element_type=F32)
                dq = scale * lax.dot_general(
                    dscores, kb[h], CONTRACT_FIRST, preferred_element_type=F32
                )
                if part:
                    dq_out[h, here, :] = dq.astype(BF16)
                else:
                    dq_own[h, here, :] = dq
                return inner

            lax.fori_loop(0, blocks, one_block, 0)
            if part:
                to_partner(dq_out.at[h], dq_in.at[h], part_send.at[0], part_recv.at[h])
        dkb[h] = (dk_sum[...] * scale).astype(BF16)
        dvb[h] = dv_sum[...].astype(BF16)
        send_out(dkb, dk_ref, 1, h)
        send_out(dvb, dv_ref, 2, h)

    def finish(h):
        part = dq_in.at[h]
        pltpu.make_async_copy(part, part, part_recv.at[h]).wait()
        dqb[h] = (dq_own[h] + dq_in[h].astype(F32)).astype(BF16)
        send_out(dqb, dq_ref, 0, h)

    ahead, lag = min(3, heads), min(2, heads)
    lax.fori_loop(0, ahead, relay_grad, 0)
    statistics(0)

    def step(h, carry):
        @pl.when(h + ahead < heads)
        def _():
            relay_grad(h + ahead, 0)

        @pl.when(h + 1 < heads)
        def _():
            statistics(h + 1)

        gradients(h)

        @pl.when(h >= lag)
        def _():
            finish(h - lag)

        return carry

    lax.fori_loop(0, heads, step, 0)

    def last(h, carry):
        finish(h)
        return carry

    lax.fori_loop(heads - lag, heads, last, 0)

    sent = grad_rows.at[:, pl.ds(0, (half - 1) * local)]
    for index in range(4):
        pltpu.make_async_copy(sent, sent, in_send.at[index]).wait()
    for index in range(2):
        pltpu.make_async_copy(dq_out, dq_out, pair_send.at[index]).wait()
    pltpu.make_async_copy(dq_out, dq_out, part_send.at[0]).wait()
    pltpu.make_async_copy(my_stats, my_stats, stat_send.at[0]).wait()
    for index, target in enumerate((dq_ref, dk_ref, dv_ref)):
        pltpu.make_async_copy(sent, sent, out_send.at[index]).wait()
        pltpu.make_async_copy(target, target, out_recv.at[index]).wait()


def per_device(dout, destination, q_bag, k_bag, v_bag, seq_ids):
    rows, width = dout.shape
    bags = lax.axis_size("bag")
    groups = lax.axis_size("head")
    half = groups // 2
    bag_rows = rows * groups
    half_rows = rows * half
    heads = width // HEAD_DIM // half
    early = (heads + 2) // 3
    block = min(256, half_rows)
    labels = jnp.broadcast_to(destination[None, :], (8, rows))
    whole = pl.BlockSpec(memory_space=pltpu.VMEM)
    far = pl.BlockSpec(memory_space=pl.ANY)
    sems = pltpu.SemaphoreType.DMA
    one = pltpu.VMEM((heads, half_rows, HEAD_DIM), BF16)
    two = pltpu.VMEM((2, heads, half_rows, HEAD_DIM), BF16)
    return pl.pallas_call(
        functools.partial(kernel, bags, groups, heads, early, block),
        out_shape=[jax.ShapeDtypeStruct((rows, width), BF16)] * 3,
        in_specs=[whole, whole, far, far, far, whole, whole],
        out_specs=[far, far, far],
        scratch_shapes=[
            pltpu.VMEM((bags, CAP, width), BF16),
            pltpu.VMEM((bags - 1, CAP, width), BF16),
            pltpu.VMEM((bags - 1, 8, rows), jnp.int32),
            pltpu.VMEM((rows, width), BF16),
            two,
            two,
            one,
            one,
            pltpu.VMEM((heads, half_rows, HEAD_DIM), F32),
            one,
            one,
            one,
            one,
            one,
            pltpu.VMEM((heads, 8, bag_rows), F32),
            pltpu.VMEM((heads, 8, bag_rows), F32),
            pltpu.VMEM((half_rows, HEAD_DIM), F32),
            pltpu.VMEM((half_rows, HEAD_DIM), F32),
            sems((4,)),
            sems((4, heads)),
            sems((2,)),
            sems((2, heads)),
            sems((1,)),
            sems((heads,)),
            sems((1,)),
            sems((heads,)),
            sems((3,)),
            sems((3,)),
            sems((bags - 1,)),
            sems((bags - 1,)),
            sems((bags - 1,)),
            sems((bags - 1,)),
        ],
        compiler_params=pltpu.CompilerParams(
            collective_id=0, has_side_effects=True, vmem_limit_bytes=56 * 1024 * 1024
        ),
    )(dout, labels, q_bag, k_bag, v_bag, seq_ids, seq_ids.reshape(bag_rows, 1))


def solution(mesh):
    placed = (
        P(("bag", "head"), None),
        P(("bag", "head")),
        P(("bag", "head"), None),
        P(("bag", "head"), None),
        P(("bag", "head"), None),
        P("bag", None),
    )
    return jax.shard_map(
        per_device,
        mesh=mesh,
        in_specs=placed,
        out_specs=(P(("bag", "head"), None),) * 3,
        check_vma=False,
    )
```

time: 254 us -> 273 us (1.075)
  Pallas kernels: 244 us -> 263 us
    pallas_call x1, Pallas kernels: 244 us -> 263 us  [per_device(): pl.pallas_call(functools.partial(kernel, bags, groups, heads, early, bloc...]
where the time goes in v1:
time: 273 us; the launch traced here: 272 us
  Pallas kernels  263 us (96%)
  local copies, waits for them, and re-layouts  8.88 us (3%)
    pallas_call x1, Pallas kernels, per_device(): pl.pallas_call(functools.partial(kernel, bags, groups, heads, early, bloc...  263 us
    unnamed x7, local copies, waits for them, and re-layouts  5.93 us

profile of v1, /device:TPU:0, one launch (start us, length us, event | category | flops | bytes accessed | tf_op | source)
XLA Modules:
  0.0 272.2 jit_solution(7096209296660905916)
XLA Ops:
  0.6 1.2 broadcast_in_dim.2.labels_ref
  1.9 1.7 copy.9.seq_col_ref
  3.6 262.7 %shard_map.85 = (bf16[128,6144]{1,0:T(8,128)(2,1)}, bf16[128,6144]{1,0:T(8,128)(2,1)}, bf16[128,6144]{1,0:T(8,128)(2,1)}) custom-call(bf16[128,6144]{1,0:T(8,128)(2,1)} %dout_ref.1, s32[8,128]{1,0:T(8,128)} %broadcast_in_dim.2.labels_ref, bf16[128,6144]{1,0:T(8,128)(2,1)} %q_ref.1, bf16[128,6144]{1,0:T(8,128)(2,1)} %k_ref.1, bf16[128,6144]{1,0:T(8,128)(2,1)} %v_ref.1, ...), custom_call_target="tpu_custom_call" | custom-call | tf_op jit(solution)/shard_map/pallas_call | solution.py:398
  266.3 0.0 copy-start.1
  266.3 2.8 %copy.13 = bf16[128,6144]{1,0:T(8,128)(2,1)} copy(bf16[128,6144]{1,0:T(8,128)(2,1)} %get-tuple-element.6) | data formatting | bytes 3145728
  269.1 0.0 copy-done.1
  269.1 0.0 copy-start
  269.1 1.1 copy.14
  270.2 0.8 copy-done
  271.1 1.1 copy.15
Async XLA Ops:
  266.3 2.8 %copy-start.1 = (bf16[128,6144]{1,0:T(8,128)(2,1)S(1)}, bf16[128,6144]{1,0:T(8,128)(2,1)}, u32[]{:S(2)}) copy-start(bf16[128,6144]{1,0:T(8,128)(2,1)} %get-tuple-element.7) | copy-start | bytes 4718596
  269.1 2.0 copy-start

commit v2 on v0

--- a/solution.py
+++ b/solution.py
@@ -39,12 +39,11 @@
     early,
     block,
     dout_ref,
-    labels_ref,
+    home_ref,
     q_ref,
     k_ref,
     v_ref,
     seq_row_ref,
-    seq_col_ref,
     dq_ref,
     dk_ref,
     dv_ref,
@@ -61,6 +60,8 @@
     dvb,
     dk_sum,
     dv_sum,
+    labels_ref,
+    seq_col_ref,
     in_send,
     in_recv,
     out_send,
@@ -113,6 +114,16 @@
         return carry
 
     lax.fori_loop(0, 1, send_qkv, 0)
+
+    labels_ref[...] = jnp.broadcast_to(home_ref[...], labels_ref.shape)
+    diagonal = lax.broadcasted_iota(jnp.int32, (rows, rows), 0) == lax.broadcasted_iota(
+        jnp.int32, (rows, rows), 1
+    )
+    for g in range(groups):
+        span = pl.ds(g * rows, rows)
+        seq_col_ref[span, :] = jnp.sum(
+            jnp.where(diagonal, seq_row_ref[:, span], 0), axis=1, keepdims=True
+        )
 
     label_copies, bag_copies = [], []
     labels = labels_ref[...]
@@ -261,7 +272,6 @@
     heads = width // HEAD_DIM // groups
     early = (heads + 1) // 2
     block = min(256, bag_rows)
-    labels = jnp.broadcast_to(destination[None, :], (8, rows))
     whole = pl.BlockSpec(memory_space=pltpu.VMEM)
     far = pl.BlockSpec(memory_space=pl.ANY)
     sems = pltpu.SemaphoreType.DMA
@@ -269,7 +279,7 @@
     return pl.pallas_call(
         functools.partial(kernel, bags, groups, heads, early, block),
         out_shape=[jax.ShapeDtypeStruct((rows, width), BF16)] * 3,
-        in_specs=[whole, whole, far, far, far, whole, whole],
+        in_specs=[whole, whole, far, far, far, whole],
         out_specs=[far, far, far],
         scratch_shapes=[
             pltpu.VMEM((bags, CAP, width), BF16),
@@ -281,6 +291,8 @@
         + [
             pltpu.VMEM((bag_rows, HEAD_DIM), F32),
             pltpu.VMEM((bag_rows, HEAD_DIM), F32),
+            pltpu.VMEM((8, rows), jnp.int32),
+            pltpu.VMEM((bag_rows, 1), jnp.int32),
             sems((4,)),
             sems((4, heads)),
             sems((3,)),
@@ -293,7 +305,7 @@
         compiler_params=pltpu.CompilerParams(
             collective_id=0, has_side_effects=True, vmem_limit_bytes=56 * 1024 * 1024
         ),
-    )(dout, labels, q_bag, k_bag, v_bag, seq_ids, seq_ids.reshape(bag_rows, 1))
+    )(dout, destination[None, :], q_bag, k_bag, v_bag, seq_ids)
 
 
 def solution(mesh):

time: 254 us -> 251 us (0.988)
  local copies, waits for them, and re-layouts: 8.88 us -> 5.93 us
where the time goes in v2:
time: 251 us
  Pallas kernels  244 us (97%)
  local copies, waits for them, and re-layouts  5.93 us (2%)
    pallas_call x1, Pallas kernels, per_device(): pl.pallas_call(functools.partial(kernel, bags, groups, heads, early, bloc...  244 us
    unnamed x7, local copies, waits for them, and re-layouts  5.93 us

profile of v2, /device:TPU:0, one launch (start us, length us, event | category | flops | bytes accessed | tf_op | source)
XLA Modules:
  0.0 250.6 jit_solution(18026563459991218264)
XLA Ops:
  0.6 244.0 %shard_map.85 = (bf16[128,6144]{1,0:T(8,128)(2,1)}, bf16[128,6144]{1,0:T(8,128)(2,1)}, bf16[128,6144]{1,0:T(8,128)(2,1)}) custom-call(bf16[128,6144]{1,0:T(8,128)(2,1)} %dout_ref.1, s32[1,128]{1,0:T(1,128)} %bitcast.1, bf16[128,6144]{1,0:T(8,128)(2,1)} %q_ref.1, bf16[128,6144]{1,0:T(8,128)(2,1)} %k_ref.1, bf16[128,6144]{1,0:T(8,128)(2,1)} %v_ref.1, ...), custom_call_target="tpu_custom_call" | custom-call | tf_op jit(solution)/shard_map/pallas_call | solution.py:279
  244.7 0.0 copy-start.1
  244.7 2.8 %copy.12 = bf16[128,6144]{1,0:T(8,128)(2,1)} copy(bf16[128,6144]{1,0:T(8,128)(2,1)} %get-tuple-element.6) | data formatting | bytes 3145728
  247.5 0.0 copy-done.1
  247.5 0.0 copy-start
  247.5 1.1 copy.13
  248.6 0.8 copy-done
  249.5 1.1 copy.14
Async XLA Ops:
  244.7 2.8 %copy-start.1 = (bf16[128,6144]{1,0:T(8,128)(2,1)S(1)}, bf16[128,6144]{1,0:T(8,128)(2,1)}, u32[]{:S(2)}) copy-start(bf16[128,6144]{1,0:T(8,128)(2,1)} %get-tuple-element.7) | copy-start | bytes 4718596
  247.5 2.0 copy-start
